TPU v7x, 32 devices: a whole 2x2x4 slice. The times are simulated.
32 devices in a mesh: band: 4 (over y, x), tile: 8 (over z, core).
Axes of the slice: x: 2, y: 2, z: 4, core: 2. Of those that a mesh axis runs over, the one named last changes fastest.
Arguments:
- image: float32 [432, 384, 512], P('band', 'tile'), may hold values from -60 to 60
Outputs:
- diffused: float32 [432, 384, 512], P('band', 'tile')
All inputs are finite; a program needn't handle non-finite values.
Results may differ from a plain program's by a relative error of at most 0.0001.
Values sent between devices are 32-bit elements; how exact they have to be, the bound alone decides.
A program may use at most 128 MiB of HBM per device.

v0:
```python
import jax
import jax.numpy as jnp
from jax import lax
from jax.sharding import PartitionSpec as P

ITERS = 3


SMOOTH = (1.0 / 64.0, 6.0 / 64.0, 15.0 / 64.0, 20.0 / 64.0, 15.0 / 64.0, 6.0 / 64.0, 1.0 / 64.0)
STEP_SIZE = 0.25
KAPPA = 0.04
EPSILON = 1e-06


def with_halo(cells, sides, width):
    for axis, dim in sides:
        count = lax.axis_size(axis)
        ends = count - 1
        head = lax.slice_in_dim(cells, 0, width, axis=dim)
        tail = lax.slice_in_dim(cells, cells.shape[dim] - width, cells.shape[dim], axis=dim)
        cells = jnp.concatenate(
            [
                lax.ppermute(tail, axis, [(i, (i + 1) % count) for i in range(ends)]),
                cells,
                lax.ppermute(head, axis, [((i + 1) % count, i) for i in range(ends)]),
            ],
            axis=dim,
        )
    return cells


def smooth_rows(field, rows):
    return sum((SMOOTH[k] * field[:, k : k + rows, :] for k in range(7)))


def smooth_columns(field):
    columns = field.shape[2]
    padded = jnp.pad(field, ((0, 0), (0, 0), (3, 3)))
    return sum((SMOOTH[k] * padded[:, :, k : k + columns] for k in range(7)))


def partial_tensor(extended):
    padded = jnp.pad(extended, ((0, 0), (0, 0), (1, 1)))
    grad_cols = (padded[:, 1:-1, 2:] - padded[:, 1:-1, :-2]) * 0.5
    grad_rows = (extended[:, 2:, :] - extended[:, :-2, :]) * 0.5
    return jnp.stack(
        [
            jnp.sum(grad_cols * grad_cols, axis=0),
            jnp.sum(grad_cols * grad_rows, axis=0),
            jnp.sum(grad_rows * grad_rows, axis=0),
        ]
    )


def tensor_of(smoothed):
    s_xx, s_xy, s_yy = (smoothed[0], smoothed[1], smoothed[2])
    trace = s_xx + s_yy
    half = (s_xx - s_yy) * 0.5
    norm_value = jnp.sqrt(4.0 * half * half + 4.0 * s_xy * s_xy + KAPPA)
    f_minus = 1.0 / jnp.sqrt(1.0 + trace)
    f_plus = 1.0 / (1.0 + trace)
    mean_f = (f_minus + f_plus) * 0.5
    gap_f = f_plus - f_minus
    return (
        mean_f + gap_f * half / norm_value,
        gap_f * s_xy / norm_value,
        mean_f - gap_f * half / norm_value,
    )


def diffusion_update(extended, rows, bands):
    partial_value = partial_tensor(extended)
    summed = lax.psum(partial_value, "band") / bands
    widened = with_halo(summed, (("tile", 1),), 3)
    smoothed = smooth_columns(smooth_rows(widened, rows))
    t_xx, t_xy, t_yy = tensor_of(smoothed)
    center = extended[:, 1:-1, :]
    padded = jnp.pad(extended, ((0, 0), (0, 0), (1, 1)))
    second_cols = padded[:, 1:-1, 2:] - 2.0 * center + padded[:, 1:-1, :-2]
    second_rows = extended[:, 2:, :] - 2.0 * center + extended[:, :-2, :]
    second_mixed = (
        padded[:, 2:, 2:] - padded[:, 2:, :-2] - padded[:, :-2, 2:] + padded[:, :-2, :-2]
    ) * 0.25
    return t_xx * second_cols + 2.0 * t_xy * second_mixed + t_yy * second_rows


def step_from(update):
    entries = float(update.size * lax.axis_size("band") * lax.axis_size("tile"))
    energy = lax.psum(jnp.sum(update * update), ("band", "tile"))
    return STEP_SIZE / jnp.sqrt(energy / entries + EPSILON)


def per_device(image):
    rows = image.shape[1]
    bands = float(image.shape[0] * lax.axis_size("band"))
    depth = 1
    current = image
    for iteration in range(ITERS):
        extended = with_halo(current, (("tile", 1),), depth)
        update = diffusion_update(extended, rows, bands)
        step_value = step_from(update)
        current = current + step_value * update
    return current


def solution(mesh):
    placed = (P("band", "tile", None),)
    return jax.shard_map(
        per_device, mesh=mesh, in_specs=placed, out_specs=P("band", "tile", None), check_vma=False
    )
```

profile of v0, /device:TPU:0, one launch (start us, length us, event | category | flops | bytes accessed | tf_op | source)
XLA Modules:
  0.0 575.0 jit_solution(2108695067812783365)
XLA Ops:
  6.5 10.2 %copy.8 = f32[108,48,512]{2,0,1:T(8,128)S(1)} copy(f32[108,48,512]{2,1,0:T(8,128)} %param.1) | data formatting | bytes 21233664 | tf_op args[0]
  16.8 1.3 collective-permute-start.1
  18.1 3.0 collective-permute-start
  21.1 1.1 collective-permute-done
  22.2 9.7 %select_maximum_fusion.4 = f32[108,50,514]{2,0,1:T(8,128)S(1)} fusion(f32[108,1,512]{2,0,1:T(8,128)S(1)} %collective-permute-done.1, f32[108,48,512]{2,0,1:T(8,128)} %copy-done.5, f32[108,1,512]{2,0,1:T(8,128)S(1)} %collective-permute-done), kind=kLoop, calls=%fused_computation.6 | loop fusion | flops 22204800 | bytes 22161600 | tf_op jit(solution)/shard_map/concatenate | solution.py:21
  31.9 16.5 %multiply_reduce_fusion.11 = (f32[48,512]{1,0:T(8,128)S(1)}, f32[48,512]{1,0:T(8,128)S(1)}, f32[48,512]{1,0:T(8,128)S(1)}) fusion(f32[108,50,514]{2,0,1:T(8,128)S(1)} %select_maximum_fusion.4, f32[108,48,512]{2,0,1:T(8,128)} %copy-done.5, f32[108,1,512]{2,0,1:T(8,128)S(1)} %collective-permute-done, f32[108,1,512]{2,0,1:T(8,128)S(1)} %collective-permute-done.1), kind=kLoop, calls=%fused_computation.52 | loop fusion | flops 31776768 | bytes 32587776 | tf_op jit(solution)/shard_map/reduce_sum | solution.py:48
  48.5 0.7 pad_maximum_fusion.12
  49.3 50.0 %all-reduce.10.cloned.1.call-done = f32[3,48,512]{2,1,0:T(8,128)} async-done(((f32[3,48,512]{2,1,0:T(8,128)}), f32[3,48,512]{2,1,0:T(8,128)}) %all-reduce.10.cloned.1.call-update) | async-done | bytes 294928 | tf_op jit(solution)/shard_map/psum | solution.py:73
  99.2 1.0 broadcast_multiply_fusion.2
  100.2 1.3 collective-permute-start.2
  101.6 1.5 collective-permute-start.3
  103.1 3.5 collective-permute-done.3
  106.6 1.2 fusion.41
  107.8 0.5 fusion.58
  108.4 39.9 %multiply_reduce_fusion.8 = (f32[]{:T(128)}, f32[108,48,512]{2,0,1:T(8,128)}) fusion(f32[108,48,512]{2,0,1:T(8,128)} %copy-done.5, f32[108,1,512]{2,0,1:T(8,128)S(1)} %collective-permute-done, f32[108,1,512]{2,0,1:T(8,128)S(1)} %collective-permute-done.1, f32[48,512]{1,0:T(8,128)S(1)} %get-tuple-element.38, f32[48,512]{1,0:T(8,128)S(1)} %get-tuple-element.37, ...), kind=kLoop, calls=%fused_computation.48 | loop fusion | flops 45121536 | bytes 85671936 | tf_op jit(solution)/shard_map/reduce_sum | solution.py:89
  148.3 41.5 %psum.43 = f32[]{:T(128)} all-reduce(f32[]{:T(128)} %get-tuple-element.18), channel_id=1, replica_groups=mesh['band'=4,'tile'=8] {'band','tile'}, use_global_device_ids=true, to_apply=%region_5.6 | all-reduce | flops 1 | bytes 8 | tf_op jit(solution)/shard_map/psum | solution.py:89
  190.5 11.8 %multiply_add_fusion.2 = f32[108,48,512]{2,0,1:T(8,128)S(1)} fusion(f32[108,48,512]{2,0,1:T(8,128)} %get-tuple-element.19, f32[]{:T(128)S(6)} %div.83, f32[108,48,512]{2,1,0:T(8,128)} %param.1), kind=kLoop, calls=%fused_computation.47 | loop fusion | flops 5308416 | bytes 31850500 | tf_op jit(solution)/shard_map/add | solution.py:102
  202.4 1.3 collective-permute-start.5
  203.7 3.4 collective-permute-start.4
  207.2 0.7 collective-permute-done.4
  207.8 8.0 %select_maximum_fusion.2 = f32[108,50,514]{2,0,1:T(8,128)S(1)} fusion(f32[108,1,512]{2,0,1:T(8,128)S(1)} %collective-permute-done.5, f32[108,48,512]{2,0,1:T(8,128)S(1)} %multiply_add_fusion.2, f32[108,1,512]{2,0,1:T(8,128)S(1)} %collective-permute-done.4), kind=kLoop, calls=%fused_computation.4 | loop fusion | flops 22204800 | bytes 22161600 | tf_op jit(solution)/shard_map/concatenate | solution.py:21
  215.8 16.5 %multiply_reduce_fusion.7 = (f32[48,512]{1,0:T(8,128)S(1)}, f32[48,512]{1,0:T(8,128)S(1)}, f32[48,512]{1,0:T(8,128)S(1)}) fusion(f32[108,50,514]{2,0,1:T(8,128)S(1)} %select_maximum_fusion.2, f32[108,48,512]{2,0,1:T(8,128)} %copy-done.4, f32[108,1,512]{2,0,1:T(8,128)S(1)} %collective-permute-done.4, f32[108,1,512]{2,0,1:T(8,128)S(1)} %collective-permute-done.5), kind=kLoop, calls=%fused_computation.45 | loop fusion | flops 31776768 | bytes 32587776 | tf_op jit(solution)/shard_map/reduce_sum | solution.py:48
  232.4 0.7 pad_maximum_fusion.13
  233.2 47.2 %all-reduce.12.cloned.1.call-done = f32[3,48,512]{2,1,0:T(8,128)} async-done(((f32[3,48,512]{2,1,0:T(8,128)}), f32[3,48,512]{2,1,0:T(8,128)}) %all-reduce.12.cloned.1.call-update) | async-done | bytes 294928 | tf_op jit(solution)/shard_map/psum | solution.py:73
  280.4 1.0 broadcast_multiply_fusion.1
  281.4 1.3 collective-permute-start.6
  282.8 1.3 collective-permute-start.7
  284.1 3.5 collective-permute-done.7
  287.5 1.2 fusion.27
  289.4 39.9 %multiply_reduce_fusion.4 = (f32[]{:T(128)}, f32[108,48,512]{2,0,1:T(8,128)}) fusion(f32[108,48,512]{2,0,1:T(8,128)} %copy-done.4, f32[108,1,512]{2,0,1:T(8,128)S(1)} %collective-permute-done.4, f32[108,1,512]{2,0,1:T(8,128)S(1)} %collective-permute-done.5, f32[48,512]{1,0:T(8,128)S(1)} %get-tuple-element.33, f32[48,512]{1,0:T(8,128)S(1)} %get-tuple-element.32, ...), kind=kLoop, calls=%fused_computation.41 | loop fusion | flops 45121536 | bytes 85671936 | tf_op jit(solution)/shard_map/reduce_sum | solution.py:89
  329.3 41.5 %psum.45 = f32[]{:T(128)} all-reduce(f32[]{:T(128)} %get-tuple-element.16), channel_id=1, replica_groups=mesh['band'=4,'tile'=8] {'band','tile'}, use_global_device_ids=true, to_apply=%region_11.12 | all-reduce | flops 1 | bytes 8 | tf_op jit(solution)/shard_map/psum | solution.py:89
  371.5 8.5 %multiply_add_fusion.1 = f32[108,48,512]{2,0,1:T(8,128)S(1)} fusion(f32[108,48,512]{2,0,1:T(8,128)} %copy-done.4, f32[108,48,512]{2,0,1:T(8,128)} %get-tuple-element.17, f32[]{:T(128)S(6)} %div.89), kind=kLoop, calls=%fused_computation.40 | loop fusion | flops 5308416 | bytes 31850500 | tf_op jit(solution)/shard_map/add | solution.py:102
  380.0 1.3 collective-permute-start.9
  381.3 3.2 collective-permute-start.8
  384.6 0.9 collective-permute-done.8
  385.5 8.0 %select_maximum_fusion = f32[108,50,514]{2,0,1:T(8,128)S(1)} fusion(f32[108,1,512]{2,0,1:T(8,128)S(1)} %collective-permute-done.9, f32[108,48,512]{2,0,1:T(8,128)S(1)} %multiply_add_fusion.1, f32[108,1,512]{2,0,1:T(8,128)S(1)} %collective-permute-done.8), kind=kLoop, calls=%fused_computation.2 | loop fusion | flops 22204800 | bytes 22161600 | tf_op jit(solution)/shard_map/concatenate | solution.py:21
  393.5 16.5 %multiply_reduce_fusion.3 = (f32[48,512]{1,0:T(8,128)S(1)}, f32[48,512]{1,0:T(8,128)S(1)}, f32[48,512]{1,0:T(8,128)S(1)}) fusion(f32[108,50,514]{2,0,1:T(8,128)S(1)} %select_maximum_fusion, f32[108,48,512]{2,0,1:T(8,128)} %copy-done.3, f32[108,1,512]{2,0,1:T(8,128)S(1)} %collective-permute-done.8, f32[108,1,512]{2,0,1:T(8,128)S(1)} %collective-permute-done.9), kind=kLoop, calls=%fused_computation.38 | loop fusion | flops 31776768 | bytes 32587776 | tf_op jit(solution)/shard_map/reduce_sum | solution.py:48
  410.0 0.7 pad_maximum_fusion.14
  410.7 47.3 %all-reduce.14.cloned.1.call-done = f32[3,48,512]{2,1,0:T(8,128)} async-done(((f32[3,48,512]{2,1,0:T(8,128)}), f32[3,48,512]{2,1,0:T(8,128)}) %all-reduce.14.cloned.1.call-update) | async-done | bytes 294928 | tf_op jit(solution)/shard_map/psum | solution.py:73
  458.1 1.0 broadcast_multiply_fusion
  459.1 1.3 collective-permute-start.10
  460.4 1.3 collective-permute-start.11
  461.7 3.5 collective-permute-done.11
  465.2 1.2 fusion.13
  467.0 39.9 %multiply_reduce_fusion = (f32[]{:T(128)}, f32[108,48,512]{2,0,1:T(8,128)}) fusion(f32[108,48,512]{2,0,1:T(8,128)} %copy-done.3, f32[108,1,512]{2,0,1:T(8,128)S(1)} %collective-permute-done.8, f32[108,1,512]{2,0,1:T(8,128)S(1)} %collective-permute-done.9, f32[48,512]{1,0:T(8,128)S(1)} %get-tuple-element.28, f32[48,512]{1,0:T(8,128)S(1)} %get-tuple-element.27, ...), kind=kLoop, calls=%fused_computation.34 | loop fusion | flops 45121536 | bytes 85671936 | tf_op jit(solution)/shard_map/reduce_sum | solution.py:89
  506.9 41.7 %psum.47 = f32[]{:T(128)} all-reduce(f32[]{:T(128)} %get-tuple-element.14), channel_id=1, replica_groups=mesh['band'=4,'tile'=8] {'band','tile'}, use_global_device_ids=true, to_apply=%region_17.18 | all-reduce | flops 1 | bytes 8 | tf_op jit(solution)/shard_map/psum | solution.py:89
  549.3 8.6 %multiply_add_fusion = f32[108,48,512]{2,0,1:T(8,128)S(1)} fusion(f32[108,48,512]{2,0,1:T(8,128)} %copy-done.3, f32[108,48,512]{2,0,1:T(8,128)} %get-tuple-element.15, f32[]{:T(128)S(6)} %div.95), kind=kLoop, calls=%fused_computation.33 | loop fusion | flops 5308416 | bytes 31850500 | tf_op jit(solution)/shard_map/add | solution.py:102
  557.9 10.3 %copy.9 = f32[108,48,512]{2,1,0:T(8,128)} copy(f32[108,48,512]{2,0,1:T(8,128)S(1)} %multiply_add_fusion) | data formatting | bytes 21233664 | tf_op jit(solution)/shard_map/add | solution.py:102
  (35 shorter events, 1.6 us)
Async XLA Ops:
  6.5 92.7 %all-reduce.10.cloned.1.call-start = ((), (), s32[]{:S(2)}) async-start(), calls=%async_computation | async-start | bytes 589824 | tf_op jit(solution)/shard_map/psum | solution.py:73
  16.7 4.4 copy-start.5
  16.8 4.4 collective-permute-start.1
  18.1 4.1 collective-permute-start
  31.9 16.5 %copy-start = (f32[108,50,514]{2,0,1:T(8,128)}, f32[108,50,514]{2,0,1:T(8,128)S(1)}, u32[]{:S(2)}) copy-start(f32[108,50,514]{2,0,1:T(8,128)S(1)} %select_maximum_fusion.4) | copy-start | bytes 33307204
  49.2 231.2 %all-reduce.12.cloned.1.call-start = ((), (), s32[]{:S(2)}) async-start(), calls=%async_computation.1 | async-start | bytes 589824 | tf_op jit(solution)/shard_map/psum | solution.py:73
  100.2 2.8 collective-permute-start.2
  101.6 5.0 collective-permute-start.3
  202.4 5.5 copy-start.4
  202.4 4.8 collective-permute-start.5
  203.7 4.1 collective-permute-start.4
  215.8 16.5 %copy-start.1 = (f32[108,50,514]{2,0,1:T(8,128)}, f32[108,50,514]{2,0,1:T(8,128)S(1)}, u32[]{:S(2)}) copy-start(f32[108,50,514]{2,0,1:T(8,128)S(1)} %select_maximum_fusion.2) | copy-start | bytes 33307204
  233.1 224.9 %all-reduce.14.cloned.1.call-start = ((), (), s32[]{:S(2)}) async-start(), calls=%async_computation.2 | async-start | bytes 589824 | tf_op jit(solution)/shard_map/psum | solution.py:73
  281.4 2.6 collective-permute-start.6
  282.8 4.8 collective-permute-start.7
  380.0 5.5 copy-start.3
  380.0 4.5 collective-permute-start.9
  381.3 4.1 collective-permute-start.8
  393.4 16.5 %copy-start.2 = (f32[108,50,514]{2,0,1:T(8,128)}, f32[108,50,514]{2,0,1:T(8,128)S(1)}, u32[]{:S(2)}) copy-start(f32[108,50,514]{2,0,1:T(8,128)S(1)} %select_maximum_fusion) | copy-start | bytes 33307204
  459.1 2.6 collective-permute-start.10
  460.4 4.8 collective-permute-start.11
Sparse Core Ops, SparseCore 0:
  49.3 49.8 all-reduce.9
  233.2 47.1 all-reduce.11
  410.9 47.1 all-reduce.13
where the time goes:
time: 584 us; the launch traced here: 575 us
  other arithmetic  235 us (40%)
  waiting for transfers between devices  158 us (27%)
  blocking collectives  125 us (21%)
  starting transfers between devices  21.7 us (4%)
  local copies, waits for them, and re-layouts  20.6 us (4%)
  between operations  15.8 us (3%)
    psum x3, waiting for transfers between devices, diffusion_update(): summed = lax.psum(partial_value, 'band') / bands  145 us
    psum x3, blocking collectives, step_from(): energy = lax.psum(jnp.sum(update * update), ('band', 'tile'))  125 us
    reduce_sum x3, other arithmetic, step_from(): energy = lax.psum(jnp.sum(update * update), ('band', 'tile'))  120 us
    reduce_sum x3, other arithmetic, partial_tensor(): jnp.sum(grad_cols * grad_cols, axis=0)  49.5 us
    add x3, other arithmetic, per_device(): current = current + step_value * update  28.9 us
    concatenate x3, other arithmetic, with_halo(): jnp.concatenate([lax.ppermute(tail, axis, [(i, (i + 1) % count) for i in...  25.6 us
    ppermute x6, starting transfers between devices, with_halo(): lax.ppermute(tail, axis, [(i, (i + 1) % count) for i in range(ends)])  13.7 us
  transfers between devices with their start and end apart: 15, of which 9 were waited for; matrix products, arithmetic and copies ran while one was open for 0% of the time, Pallas kernels for 0%

commit v1 on v0

v1 whole, which is shorter than its diff:
```python
import functools

import jax
import jax.numpy as jnp
from jax import lax
from jax.experimental import pallas as pl
from jax.experimental.pallas import tpu as pltpu
from jax.sharding import PartitionSpec as P

ITERS = 3
LANES = 128
SMOOTH = (1.0 / 64.0, 6.0 / 64.0, 15.0 / 64.0, 20.0 / 64.0, 15.0 / 64.0, 6.0 / 64.0, 1.0 / 64.0)
STEP_SIZE = 0.25
KAPPA = 0.04
EPSILON = 1e-06


def shifted(pieces, lane, by):
    count = len(pieces)
    turned = [pltpu.roll(p, (-by) % LANES, 1) for p in pieces]
    edge = lane == (LANES - 1 if by == 1 else 0)
    zero = jnp.zeros_like(pieces[0])
    out = []
    for j in range(count):
        k = j + by
        out.append(jnp.where(edge, turned[k] if 0 <= k < count else zero, turned[j]))
    return out


def with_halo(cells, sides, width):
    for axis, dim in sides:
        count = lax.axis_size(axis)
        ends = count - 1
        head = lax.slice_in_dim(cells, 0, width, axis=dim)
        tail = lax.slice_in_dim(cells, cells.shape[dim] - width, cells.shape[dim], axis=dim)
        cells = jnp.concatenate(
            [
                lax.ppermute(tail, axis, [(i, (i + 1) % count) for i in range(ends)]),
                cells,
                lax.ppermute(head, axis, [((i + 1) % count, i) for i in range(ends)]),
            ],
            axis=dim,
        )
    return cells


def smooth_rows(field, rows):
    return sum((SMOOTH[k] * field[:, k : k + rows, :] for k in range(7)))


def smooth_columns(field):
    columns = field.shape[2]
    padded = jnp.pad(field, ((0, 0), (0, 0), (3, 3)))
    return sum((SMOOTH[k] * padded[:, :, k : k + columns] for k in range(7)))


def tensor_of(smoothed):
    s_xx, s_xy, s_yy = (smoothed[0], smoothed[1], smoothed[2])
    trace = s_xx + s_yy
    half = (s_xx - s_yy) * 0.5
    norm_value = jnp.sqrt(4.0 * half * half + 4.0 * s_xy * s_xy + KAPPA)
    f_minus = 1.0 / jnp.sqrt(1.0 + trace)
    f_plus = 1.0 / (1.0 + trace)
    mean_f = (f_minus + f_plus) * 0.5
    gap_f = f_plus - f_minus
    return (
        mean_f + gap_f * half / norm_value,
        gap_f * s_xy / norm_value,
        mean_f - gap_f * half / norm_value,
    )


def neighbours(above, prev, mid, nxt, below, b, n, NC):
    i = pl.program_id(0)
    last = pl.num_programs(0) - 1
    get = lambda ref: [ref[0, pl.ds(b, n), pl.ds(j * LANES, LANES)] for j in range(NC)]
    up = [jnp.where(i == 0, x, y) for x, y in zip(get(above), get(prev))]
    down = [jnp.where(i == last, x, y) for x, y in zip(get(below), get(nxt))]
    return up, get(mid), down


def tensor_kernel(above, prev, mid_ref, nxt, below, out):
    B, W = mid_ref.shape[1:]
    NC = W // LANES
    acc = {}
    for b in range(0, B, 8):
        n = min(8, B - b)
        lane = lax.broadcasted_iota(jnp.int32, (n, LANES), 1)
        up, mid, down = neighbours(above, prev, mid_ref, nxt, below, b, n, NC)
        right, left = shifted(mid, lane, 1), shifted(mid, lane, -1)
        for j in range(NC):
            gx, gy = right[j] - left[j], down[j] - up[j]
            for c, v in enumerate((gx * gx, gx * gy, gy * gy)):
                key = (n, c, j)
                acc[key] = acc[key] + v if key in acc else v
    for c in range(3):
        for j in range(NC):
            out[0, c:c + 1, pl.ds(j * LANES, LANES)] = sum(
                jnp.sum(acc[k], axis=0, keepdims=True) for k in sorted(acc) if k[1:] == (c, j))


def update_kernel(above, prev, mid_ref, nxt, below, coef, out, energy):
    B, W = mid_ref.shape[1:]
    NC = W // LANES
    w = [[jnp.broadcast_to(coef[0, k:k + 1, pl.ds(j * LANES, LANES)], (8, LANES))
          for j in range(NC)] for k in range(6)]
    acc = {}
    for b in range(0, B, 8):
        n = min(8, B - b)
        lane = lax.broadcasted_iota(jnp.int32, (n, LANES), 1)
        up, mid, down = neighbours(above, prev, mid_ref, nxt, below, b, n, NC)
        k = [[v[:n] for v in q] for q in w]
        g = [down[j] - up[j] for j in range(NC)]
        ahead = [k[0][j] * mid[j] + k[1][j] * g[j] for j in range(NC)]
        behind = [k[2][j] * mid[j] - k[3][j] * g[j] for j in range(NC)]
        ahead, behind = shifted(ahead, lane, 1), shifted(behind, lane, -1)
        for j in range(NC):
            u = (ahead[j] + behind[j]) + (k[4][j] * (down[j] + up[j]) + k[5][j] * mid[j])
            out[0, pl.ds(b, n), pl.ds(j * LANES, LANES)] = u
            acc[n, j] = acc[n, j] + u * u if (n, j) in acc else u * u
    energy[0] = sum(jnp.sum(v, axis=0, keepdims=True) for v in acc.values())


def per_device(image):
    B, rows, W = image.shape
    NB = lax.axis_size("band")
    nt = lax.axis_size("tile")
    bands = float(B * NB)
    entries = float(B * NB * rows * nt * W)
    one = lambda index: pl.BlockSpec((1, B, W), index)
    five = [one(lambda i: (0, 0, 0)), one(lambda i: (jnp.maximum(i - 1, 0), 0, 0)),
            one(lambda i: (i, 0, 0)), one(lambda i: (jnp.minimum(i + 1, rows - 1), 0, 0)),
            one(lambda i: (0, 0, 0))]
    line = lambda k, w: pl.BlockSpec((1, k, w), lambda i: (i, 0, 0))
    shape = lambda *s: jax.ShapeDtypeStruct(s, jnp.float32)
    params = pltpu.CompilerParams(vmem_limit_bytes=24 * 2**20)
    tensor = pl.pallas_call(tensor_kernel, grid=(rows,), in_specs=five, out_specs=line(3, W),
                            out_shape=shape(rows, 3, W), compiler_params=params, name="tensor")
    update = pl.pallas_call(update_kernel, grid=(rows,), in_specs=five + [line(6, W)],
                            out_specs=[line(B, W), line(1, LANES)],
                            out_shape=[shape(rows, B, W), shape(rows, 1, LANES)],
                            compiler_params=params, name="update")
    field = jnp.transpose(image, (1, 0, 2))
    down_pairs = [(i, i + 1) for i in range(nt - 1)]
    up_pairs = [(i + 1, i) for i in range(nt - 1)]
    ahead = lambda x: jnp.pad(x[:, 1:], ((0, 0), (0, 1)))
    behind = lambda x: jnp.pad(x[:, :-1], ((0, 0), (1, 0)))
    for _ in range(ITERS):
        above = lax.ppermute(field[rows - 1:], "tile", down_pairs)
        below = lax.ppermute(field[:1], "tile", up_pairs)
        part = tensor(above, field, field, field, below)
        part = jnp.transpose(part, (1, 0, 2))
        summed = lax.psum(part, "band") * (0.25 / bands)
        widened = with_halo(summed, (("tile", 1),), 3)
        t_xx, t_xy, t_yy = tensor_of(smooth_columns(smooth_rows(widened, rows)))
        t_xy = 0.5 * t_xy
        coef = jnp.stack([behind(t_xx), behind(t_xy), ahead(t_xx), ahead(t_xy), t_yy,
                          -2.0 * (t_xx + t_yy)], axis=1)
        change, energy = update(above, field, field, field, below, coef)
        total = lax.psum(jnp.sum(energy), ("band", "tile"))
        field = field + (STEP_SIZE / jnp.sqrt(total / entries + EPSILON)) * change
    return jnp.transpose(field, (1, 0, 2))


def solution(mesh):
    placed = (P("band", "tile", None),)
    return jax.shard_map(
        per_device, mesh=mesh, in_specs=placed, out_specs=P("band", "tile", None), check_vma=False
    )
```

time: 584 us -> 473 us (0.81); the launches traced: 575 us -> 472 us
  other arithmetic: 235 us -> 40.1 us
  Pallas kernels: 0 us -> 60.9 us
  local copies, waits for them, and re-layouts: 20.6 us -> 50.8 us
    reduce_sum x6 -> x3, other arithmetic: 169 us -> 1.95 us  [per_device(): total = lax.psum(jnp.sum(energy), ('band', 'tile'))]
    pallas_call x0 -> x6, Pallas kernels: none -> 60.9 us  [the longest x3 30.6 us: per_device(): change, energy = update(above, field, field, field, below, coef)]
    concatenate x3 -> x0, other arithmetic: 25.6 us -> none  [with_halo(): jnp.concatenate([lax.ppermute(tail, axis, [(i, (i + 1) % count) for i in...]
    unnamed x13 -> x28, local copies, waits for them, and re-layouts: 10.2 us -> 35.3 us
    ppermute x0 -> x6, starting transfers between devices: none -> 13 us  [the longest x3 9.13 us: per_device(): above = lax.ppermute(field[rows - 1:], 'tile', down_pairs)]
    add x1 -> x0, local copies, waits for them, and re-layouts: 10.3 us -> none  [per_device(): current = current + step_value * update]
    transpose x0 -> x1, local copies, waits for them, and re-layouts: none -> 10.3 us  [per_device(): return jnp.transpose(field, (1, 0, 2))]
    ppermute x6 -> x3, starting transfers between devices: 13.7 us -> 3.95 us  [with_halo(): lax.ppermute(tail, axis, [(i, (i + 1) % count) for i in range(ends)])]
where the time goes in v1:
time: 473 us; the launch traced here: 472 us
  waiting for transfers between devices  158 us (33%)
  blocking collectives  125 us (26%)
  Pallas kernels  60.9 us (13%)
  local copies, waits for them, and re-layouts  50.8 us (11%)
  other arithmetic  40.1 us (8%)
  starting transfers between devices  20.9 us (4%)
  between operations  15.8 us (3%)
    psum x3, waiting for transfers between devices, per_device(): summed = lax.psum(part, 'band') * (0.25 / bands)  145 us
    psum x3, blocking collectives, per_device(): total = lax.psum(jnp.sum(energy), ('band', 'tile'))  125 us
    unnamed x28, local copies, waits for them, and re-layouts  35.3 us
    pallas_call x3, Pallas kernels, per_device(): change, energy = update(above, field, field, field, below, coef)  30.6 us
    pallas_call x3, Pallas kernels, per_device(): part = tensor(above, field, field, field, below)  30.3 us
    add x2, other arithmetic, per_device(): field = field + STEP_SIZE / jnp.sqrt(total / entries + EPSILON) * change  20.3 us
    ppermute x3, waiting for transfers between devices, with_halo(): lax.ppermute(head, axis, [((i + 1) % count, i) for i in range(ends)])  10.4 us
    transpose x1, local copies, waits for them, and re-layouts, per_device(): return jnp.transpose(field, (1, 0, 2))  10.3 us
  transfers between devices with their start and end apart: 15, of which 9 were waited for; matrix products, arithmetic and copies ran while one was open for 0% of the time, Pallas kernels for 0%

profile of v1, /device:TPU:0, one launch (start us, length us, event | category | flops | bytes accessed | tf_op | source)
XLA Modules:
  0.0 471.6 jit_solution(7490345979387904124)
XLA Ops:
  6.5 10.2 %copy.71 = f32[108,48,512]{2,0,1:T(8,128)S(1)} copy(f32[108,48,512]{2,1,0:T(8,128)} %param.1) | data formatting | bytes 21233664 | tf_op args[0]
  16.8 1.3 collective-permute-start.1
  18.1 3.0 collective-permute-start
  21.1 1.1 collective-permute-done.above
  22.2 9.9 %tensor.3 = f32[48,3,512]{2,1,0:T(4,128)S(1)} custom-call(f32[1,108,512]{2,1,0:T(8,128)S(1)} %collective-permute-done.above, f32[48,108,512]{2,1,0:T(8,128)S(1)} %bitcast.223, f32[48,108,512]{2,1,0:T(8,128)S(1)} %bitcast.224, f32[48,108,512]{2,1,0:T(8,128)S(1)} %bitcast.225, f32[1,108,512]{2,1,0:T(8,128)S(1)} %collective-permute-done.1.below), custom_call_target="tpu_custom_call" | custom-call | tf_op jit(solution)/shard_map/tensor/pallas_call | solution.py:151
  33.0 50.0 %all-reduce.19.cloned.1.call-done = f32[3,48,512]{2,1,0:T(8,128)} async-done(((f32[3,48,512]{2,1,0:T(8,128)}), f32[3,48,512]{2,1,0:T(8,128)}) %all-reduce.19.cloned.1.call-update) | async-done | bytes 294928 | tf_op jit(solution)/shard_map/psum | solution.py:153
  82.9 1.0 broadcast_multiply_fusion.2
  84.0 1.3 collective-permute-start.2
  85.3 1.3 collective-permute-start.3
  86.6 3.5 collective-permute-done.3
  90.1 1.2 fusion.31
  92.8 4.1 copy-done.5
  96.9 10.2 %update.3 = (f32[48,108,512]{2,1,0:T(8,128)S(1)}, f32[48,1,128]{2,1,0:T(1,128)S(1)}) custom-call(f32[1,108,512]{2,1,0:T(8,128)S(1)} %collective-permute-done.above, f32[48,108,512]{2,1,0:T(8,128)S(1)} %bitcast.226, f32[48,108,512]{2,1,0:T(8,128)S(1)} %bitcast.227, f32[48,108,512]{2,1,0:T(8,128)S(1)} %bitcast.228, ...), custom_call_target="tpu_custom_call" | custom-call | tf_op jit(solution)/shard_map/update/pallas_call | solution.py:159
  107.2 4.2 copy-done.7
  112.0 41.7 %psum.43 = f32[]{:T(128)} all-reduce(f32[]{:T(128)} %reduce_sum.27), channel_id=1, replica_groups=mesh['band'=4,'tile'=8] {'band','tile'}, use_global_device_ids=true, to_apply=%region_2.3 | all-reduce | flops 1 | bytes 8 | tf_op jit(solution)/shard_map/psum | solution.py:160
  154.3 11.8 %multiply_add_fusion.1.prev.mid_ref.nxt = f32[48,108,512]{2,1,0:T(8,128)S(1)} fusion(f32[48,108,512]{2,1,0:T(8,128)} %copy-done.7, f32[]{:T(128)S(6)} %div.107, f32[108,48,512]{2,1,0:T(8,128)} %param.1), kind=kLoop, calls=%fused_computation.3 | loop fusion | flops 5308416 | bytes 31850500 | tf_op jit(solution)/shard_map/add | solution.py:161
  166.2 1.3 collective-permute-start.5
  167.5 3.0 collective-permute-start.4
  170.6 1.1 collective-permute-done.4.above
  171.7 10.2 %tensor.4 = f32[48,3,512]{2,1,0:T(4,128)S(1)} custom-call(f32[1,108,512]{2,1,0:T(8,128)S(1)} %collective-permute-done.4.above, f32[48,108,512]{2,1,0:T(8,128)S(1)} %multiply_add_fusion.1.prev.mid_ref.nxt, f32[48,108,512]{2,1,0:T(8,128)S(1)} %multiply_add_fusion.1.prev.mid_ref.nxt, f32[48,108,512]{2,1,0:T(8,128)S(1)} %multiply_add_fusion.1.prev.mid_ref.nxt, ...), custom_call_target="tpu_custom_call" | custom-call | tf_op jit(solution)/shard_map/tensor/pallas_call | solution.py:151
  182.8 47.2 %all-reduce.21.cloned.1.call-done = f32[3,48,512]{2,1,0:T(8,128)} async-done(((f32[3,48,512]{2,1,0:T(8,128)}), f32[3,48,512]{2,1,0:T(8,128)}) %all-reduce.21.cloned.1.call-update) | async-done | bytes 294928 | tf_op jit(solution)/shard_map/psum | solution.py:153
  230.0 1.0 broadcast_multiply_fusion.1
  231.0 1.3 collective-permute-start.6
  232.4 1.3 collective-permute-start.7
  233.7 3.5 collective-permute-done.7
  237.1 1.2 fusion.17
  240.0 4.1 copy-done.3
  244.1 10.2 %update.4 = (f32[48,108,512]{2,1,0:T(8,128)S(1)}, f32[48,1,128]{2,1,0:T(1,128)S(1)}) custom-call(f32[1,108,512]{2,1,0:T(8,128)S(1)} %collective-permute-done.4.above, f32[48,108,512]{2,1,0:T(8,128)S(1)} %copy-done.3, f32[48,108,512]{2,1,0:T(8,128)S(1)} %copy-done.3, f32[48,108,512]{2,1,0:T(8,128)S(1)} %copy-done.3, ...), custom_call_target="tpu_custom_call" | custom-call | tf_op jit(solution)/shard_map/update/pallas_call | solution.py:159
  254.3 4.0 copy-done.8
  259.0 41.5 %psum.45 = f32[]{:T(128)} all-reduce(f32[]{:T(128)} %reduce_sum.28), channel_id=1, replica_groups=mesh['band'=4,'tile'=8] {'band','tile'}, use_global_device_ids=true, to_apply=%region_5.6 | all-reduce | flops 1 | bytes 8 | tf_op jit(solution)/shard_map/psum | solution.py:160
  301.2 8.5 %multiply_add_fusion.prev.mid_ref.nxt = f32[48,108,512]{2,1,0:T(8,128)S(1)} fusion(f32[48,108,512]{2,1,0:T(8,128)} %copy-done.2, f32[48,108,512]{2,1,0:T(8,128)} %copy-done.8, f32[]{:T(128)S(6)} %div.113), kind=kLoop, calls=%fused_computation.2 | loop fusion | flops 5308416 | bytes 31850500 | tf_op jit(solution)/shard_map/add | solution.py:161
  309.7 1.3 collective-permute-start.9
  311.0 3.0 collective-permute-start.8
  314.1 1.1 collective-permute-done.8.above
  315.1 10.2 %tensor.5 = f32[48,3,512]{2,1,0:T(4,128)S(1)} custom-call(f32[1,108,512]{2,1,0:T(8,128)S(1)} %collective-permute-done.8.above, f32[48,108,512]{2,1,0:T(8,128)S(1)} %multiply_add_fusion.prev.mid_ref.nxt, f32[48,108,512]{2,1,0:T(8,128)S(1)} %multiply_add_fusion.prev.mid_ref.nxt, f32[48,108,512]{2,1,0:T(8,128)S(1)} %multiply_add_fusion.prev.mid_ref.nxt, ...), custom_call_target="tpu_custom_call" | custom-call | tf_op jit(solution)/shard_map/tensor/pallas_call | solution.py:151
  326.2 47.3 %all-reduce.23.cloned.1.call-done = f32[3,48,512]{2,1,0:T(8,128)} async-done(((f32[3,48,512]{2,1,0:T(8,128)}), f32[3,48,512]{2,1,0:T(8,128)}) %all-reduce.23.cloned.1.call-update) | async-done | bytes 294928 | tf_op jit(solution)/shard_map/psum | solution.py:153
  373.5 1.0 broadcast_multiply_fusion
  374.5 1.3 collective-permute-start.10
  375.9 1.3 collective-permute-start.11
  377.2 3.5 collective-permute-done.11
  380.6 1.2 fusion.3
  383.8 0.9 stack.65.coef
  384.8 4.1 copy-done.1
  388.9 10.2 %update.5 = (f32[48,108,512]{2,1,0:T(8,128)S(1)}, f32[48,1,128]{2,1,0:T(1,128)S(1)}) custom-call(f32[1,108,512]{2,1,0:T(8,128)S(1)} %collective-permute-done.8.above, f32[48,108,512]{2,1,0:T(8,128)S(1)} %copy-done.1, f32[48,108,512]{2,1,0:T(8,128)S(1)} %copy-done.1, f32[48,108,512]{2,1,0:T(8,128)S(1)} %copy-done.1, ...), custom_call_target="tpu_custom_call" | custom-call | tf_op jit(solution)/shard_map/update/pallas_call | solution.py:159
  399.1 4.0 copy-done.6
  403.8 41.7 %psum.47 = f32[]{:T(128)} all-reduce(f32[]{:T(128)} %reduce_sum.29), channel_id=1, replica_groups=mesh['band'=4,'tile'=8] {'band','tile'}, use_global_device_ids=true, to_apply=%region_8.9 | all-reduce | flops 1 | bytes 8 | tf_op jit(solution)/shard_map/psum | solution.py:160
  446.2 8.6 %add_bitcast_fusion = f32[108,48,512]{2,0,1:T(8,128)S(1)} fusion(f32[48,108,512]{2,1,0:T(8,128)} %copy-done, f32[48,108,512]{2,1,0:T(8,128)} %copy-done.6, f32[]{:T(128)S(6)} %div.119), kind=kLoop, calls=%fused_computation.1 | loop fusion | flops 5308416 | bytes 31850500 | tf_op jit(solution)/shard_map/transpose | solution.py:162
  454.8 10.3 %copy.43 = f32[108,48,512]{2,1,0:T(8,128)} copy(f32[108,48,512]{2,0,1:T(8,128)S(1)} %add_bitcast_fusion) | data formatting | bytes 21233664 | tf_op jit(solution)/shard_map/transpose | solution.py:162
  (73 shorter events, 9.5 us)
Async XLA Ops:
  6.5 76.4 %all-reduce.19.cloned.1.call-start = ((), (), s32[]{:S(2)}) async-start(), calls=%async_computation | async-start | bytes 589824 | tf_op jit(solution)/shard_map/psum | solution.py:153
  16.7 15.4 %copy-start.4 = (f32[108,48,512]{2,0,1:T(8,128)}, f32[108,48,512]{2,0,1:T(8,128)S(1)}, u32[]{:S(2)}) copy-start(f32[108,48,512]{2,0,1:T(8,128)S(1)} %copy.71) | copy-start | bytes 31850500
  16.8 4.4 collective-permute-start.1
  18.1 4.1 collective-permute-start
  32.9 197.1 %all-reduce.21.cloned.1.call-start = ((), (), s32[]{:S(2)}) async-start(), calls=%async_computation.1 | async-start | bytes 589824 | tf_op jit(solution)/shard_map/psum | solution.py:153
  84.0 2.6 collective-permute-start.2
  85.3 4.8 %collective-permute-start.3 = (f32[3,3,512]{2,1,0:T(4,128)S(1)}, f32[3,3,512]{2,1,0:T(4,128)S(1)}, u32[]{:S(2)}, u32[]{:S(2)}) collective-permute-start(f32[3,3,512]{2,1,0:T(4,128)S(1)} %get-tuple-element.39), channel_id=1, source_target_pairs={{1,0},{2,1},{3,2},{4,3},{5,4},{6,5},{7,6},{9,8},{10,9},{11,10},{12... | collective-permute-start | bytes 55304 | tf_op jit(solution)/shard_map/ppermute | solution.py:40
  92.8 4.1 copy-start.5
  107.1 4.2 copy-start.7
  166.2 15.7 %copy-start.2 = (f32[48,108,512]{2,1,0:T(8,128)}, f32[48,108,512]{2,1,0:T(8,128)S(1)}, u32[]{:S(2)}) copy-start(f32[48,108,512]{2,1,0:T(8,128)S(1)} %multiply_add_fusion.1.prev.mid_ref.nxt) | copy-start | bytes 31850500
  166.2 4.4 collective-permute-start.5
  167.5 4.1 collective-permute-start.4
  182.7 190.8 %all-reduce.23.cloned.1.call-start = ((), (), s32[]{:S(2)}) async-start(), calls=%async_computation.2 | async-start | bytes 589824 | tf_op jit(solution)/shard_map/psum | solution.py:153
  231.0 2.6 collective-permute-start.6
  232.4 4.8 %collective-permute-start.7 = (f32[3,3,512]{2,1,0:T(4,128)S(1)}, f32[3,3,512]{2,1,0:T(4,128)S(1)}, u32[]{:S(2)}, u32[]{:S(2)}) collective-permute-start(f32[3,3,512]{2,1,0:T(4,128)S(1)} %get-tuple-element.35), channel_id=1, source_target_pairs={{1,0},{2,1},{3,2},{4,3},{5,4},{6,5},{7,6},{9,8},{10,9},{11,10},{12... | collective-permute-start | bytes 55304 | tf_op jit(solution)/shard_map/ppermute | solution.py:40
  240.0 4.1 copy-start.3
  254.3 4.0 copy-start.8
  309.7 15.7 %copy-start = (f32[48,108,512]{2,1,0:T(8,128)}, f32[48,108,512]{2,1,0:T(8,128)S(1)}, u32[]{:S(2)}) copy-start(f32[48,108,512]{2,1,0:T(8,128)S(1)} %multiply_add_fusion.prev.mid_ref.nxt) | copy-start | bytes 31850500
  309.7 4.4 collective-permute-start.9
  311.0 4.1 collective-permute-start.8
  374.5 2.6 collective-permute-start.10
  375.9 4.8 %collective-permute-start.11 = (f32[3,3,512]{2,1,0:T(4,128)S(1)}, f32[3,3,512]{2,1,0:T(4,128)S(1)}, u32[]{:S(2)}, u32[]{:S(2)}) collective-permute-start(f32[3,3,512]{2,1,0:T(4,128)S(1)} %get-tuple-element.31), channel_id=1, source_target_pairs={{1,0},{2,1},{3,2},{4,3},{5,4},{6,5},{7,6},{9,8},{10,9},{11,10},{12... | collective-permute-start | bytes 55304 | tf_op jit(solution)/shard_map/ppermute | solution.py:40
  384.8 4.1 copy-start.1
  399.1 4.0 copy-start.6
Sparse Core Ops, SparseCore 0:
  33.1 49.8 all-reduce.18
  182.9 47.1 all-reduce.20
  326.3 47.1 all-reduce.22

commit v2 on v1

--- a/solution.py
+++ b/solution.py
@@ -121,6 +121,17 @@
     energy[0] = sum(jnp.sum(v, axis=0, keepdims=True) for v in acc.values())
 
 
+def total_over(x, axis):
+    count = lax.axis_size(axis)
+    if count & (count - 1):
+        return lax.psum(x, axis)
+    hop = 1
+    while hop < count:
+        x = x + lax.ppermute(x, axis, [(i, i ^ hop) for i in range(count)])
+        hop *= 2
+    return x
+
+
 def per_device(image):
     B, rows, W = image.shape
     NB = lax.axis_size("band")
@@ -150,14 +161,14 @@
         below = lax.ppermute(field[:1], "tile", up_pairs)
         part = tensor(above, field, field, field, below)
         part = jnp.transpose(part, (1, 0, 2))
-        summed = lax.psum(part, "band") * (0.25 / bands)
+        summed = total_over(part, "band") * (0.25 / bands)
         widened = with_halo(summed, (("tile", 1),), 3)
         t_xx, t_xy, t_yy = tensor_of(smooth_columns(smooth_rows(widened, rows)))
         t_xy = 0.5 * t_xy
         coef = jnp.stack([behind(t_xx), behind(t_xy), ahead(t_xx), ahead(t_xy), t_yy,
                           -2.0 * (t_xx + t_yy)], axis=1)
         change, energy = update(above, field, field, field, below, coef)
-        total = lax.psum(jnp.sum(energy), ("band", "tile"))
+        total = total_over(total_over(jnp.sum(energy, axis=(0, 1)).reshape(1, LANES), "band"), "tile").sum()
         field = field + (STEP_SIZE / jnp.sqrt(total / entries + EPSILON)) * change
     return jnp.transpose(field, (1, 0, 2))
 

time: 473 us -> 285 us (0.60)
  blocking collectives: 125 us -> 0 us
  waiting for transfers between devices: 158 us -> 81.4 us
  starting transfers between devices: 20.9 us -> 61.9 us
  between operations: 15.8 us -> 2.76 us
  local copies, waits for them, and re-layouts: 50.8 us -> 40.4 us
  other arithmetic: 40.1 us -> 34.9 us
    psum x3 -> x0, waiting for transfers between devices: 145 us -> none  [per_device(): summed = lax.psum(part, 'band') * (0.25 / bands)]
    psum x3 -> x0, blocking collectives: 125 us -> none  [per_device(): total = lax.psum(jnp.sum(energy), ('band', 'tile'))]
    ppermute x0 -> x21, waiting for transfers between devices: none -> 64.1 us  [total_over(): x = x + lax.ppermute(x, axis, [(i, i ^ hop) for i in range(count)])]
    ppermute x0 -> x21, starting transfers between devices: none -> 35.2 us  [total_over(): x = x + lax.ppermute(x, axis, [(i, i ^ hop) for i in range(count)])]
    unnamed x28 -> x22, local copies, waits for them, and re-layouts: 35.3 us -> 27 us
    ppermute x3, starting transfers between devices: 3.95 us -> 9.37 us  [with_halo(): lax.ppermute(tail, axis, [(i, (i + 1) % count) for i in range(ends)])]
  transfers between devices with their start and end apart: 15 -> 33, of which waited for: 9 -> 27; matrix products, arithmetic and copies ran while one was open for 0% -> 0% of each run, Pallas kernels for 0% -> 0%
where the time goes in v2:
time: 285 us; the launch traced here: 284 us
  waiting for transfers between devices  81.4 us (29%)
  Pallas kernels  62.8 us (22%)
  starting transfers between devices  61.9 us (22%)
  local copies, waits for them, and re-layouts  40.4 us (14%)
  other arithmetic  34.9 us (12%)
    ppermute x21, waiting for transfers between devices, total_over(): x = x + lax.ppermute(x, axis, [(i, i ^ hop) for i in range(count)])  64.1 us
    ppermute x21, starting transfers between devices, total_over(): x = x + lax.ppermute(x, axis, [(i, i ^ hop) for i in range(count)])  35.2 us
    pallas_call x3, Pallas kernels, per_device(): change, energy = update(above, field, field, field, below, coef)  31.9 us
    pallas_call x3, Pallas kernels, per_device(): part = tensor(above, field, field, field, below)  30.9 us
    unnamed x22, local copies, waits for them, and re-layouts  27 us
    add x2, other arithmetic, per_device(): field = field + STEP_SIZE / jnp.sqrt(total / entries + EPSILON) * change  20.3 us
    ppermute x3, waiting for transfers between devices, with_halo(): lax.ppermute(head, axis, [((i + 1) % count, i) for i in range(ends)])  14.1 us
    transpose x1, local copies, waits for them, and re-layouts, per_device(): return jnp.transpose(field, (1, 0, 2))  10.3 us
  transfers between devices with their start and end apart: 33, of which 27 were waited for; matrix products, arithmetic and copies ran while one was open for 0% of the time, Pallas kernels for 0%

profile of v2, /device:TPU:0, one launch (start us, length us, event | category | flops | bytes accessed | tf_op | source)
XLA Modules:
  0.0 284.1 jit_solution(11085996430357786093)
XLA Ops:
  0.0 10.2 %copy.77 = f32[108,48,512]{2,0,1:T(8,128)S(1)} copy(f32[108,48,512]{2,1,0:T(8,128)} %param.1) | data formatting | bytes 21233664 | tf_op args[0]
  11.5 3.0 %collective-permute-start = (f32[1,108,512]{2,1,0:T(8,128)S(1)}, f32[1,108,512]{2,1,0:T(8,128)S(1)}, u32[]{:S(2)}, u32[]{:S(2)}) collective-permute-start(f32[1,108,512]{2,1,0:T(8,128)S(1)} %get-tuple-element.24), channel_id=1, source_target_pairs={{0,1},{1,2},{2,3},{3,4},{4,5},{5,6},{6,7},{8,9},{9,10},{10,11},{11... | collective-permute-start | bytes 663560 | tf_op jit(solution)/shard_map/ppermute | solution.py:160
  15.7 10.2 %tensor.3 = f32[48,3,512]{2,1,0:T(4,128)S(1)} custom-call(f32[1,108,512]{2,1,0:T(8,128)S(1)} %collective-permute-done.above, f32[48,108,512]{2,1,0:T(8,128)S(1)} %bitcast.235, f32[48,108,512]{2,1,0:T(8,128)S(1)} %bitcast.236, f32[48,108,512]{2,1,0:T(8,128)S(1)} %bitcast.237, f32[1,108,512]{2,1,0:T(8,128)S(1)} %collective-permute-done.1.below), custom_call_target="tpu_custom_call" | custom-call | tf_op jit(solution)/shard_map/tensor/pallas_call | solution.py:162
  26.0 3.0 %collective-permute-start.2 = (f32[3,48,512]{2,1,0:T(8,128)S(1)}, f32[3,48,512]{2,1,0:T(8,128)S(1)}, u32[]{:S(2)}, u32[]{:S(2)}) collective-permute-start(f32[3,48,512]{2,1,0:T(8,128)S(1)} %bitcast.241), channel_id=1, source_target_pairs={{0,8},{8,0},{16,24},{24,16},{1,9},{9,1},{17,25},{25,17},{2,10},{10... | collective-permute-start | bytes 884744 | tf_op jit(solution)/shard_map/ppermute | solution.py:130
  29.0 5.3 %collective-permute-done.2 = f32[3,48,512]{2,1,0:T(8,128)S(1)} collective-permute-done((f32[3,48,512]{2,1,0:T(8,128)S(1)}, f32[3,48,512]{2,1,0:T(8,128)S(1)}, u32[]{:S(2)}, u32[]{:S(2)}) %collective-permute-start.2) | collective-permute-done | bytes 294944 | tf_op jit(solution)/shard_map/ppermute | solution.py:130
  34.3 2.6 collective-permute-start.3
  36.9 6.5 %collective-permute-done.3 = f32[3,48,512]{2,1,0:T(8,128)S(1)} collective-permute-done((f32[3,48,512]{2,1,0:T(8,128)S(1)}, f32[3,48,512]{2,1,0:T(8,128)S(1)}, u32[]{:S(2)}, u32[]{:S(2)}) %collective-permute-start.3) | collective-permute-done | bytes 294944 | tf_op jit(solution)/shard_map/ppermute | solution.py:130
  43.5 3.0 %collective-permute-start.4 = (f32[3,3,512]{2,1,0:T(4,128)S(1)}, f32[3,3,512]{2,1,0:T(4,128)S(1)}, u32[]{:S(2)}, u32[]{:S(2)}) collective-permute-start(f32[3,3,512]{2,1,0:T(4,128)S(1)} %get-tuple-element.38), channel_id=1, source_target_pairs={{0,1},{1,2},{2,3},{3,4},{4,5},{5,6},{6,7},{8,9},{9,10},{10,11},{11... | collective-permute-start | bytes 55304 | tf_op jit(solution)/shard_map/ppermute | solution.py:38
  48.1 5.0 %collective-permute-done.5 = f32[3,3,512]{2,1,0:T(4,128)S(1)} collective-permute-done((f32[3,3,512]{2,1,0:T(4,128)S(1)}, f32[3,3,512]{2,1,0:T(4,128)S(1)}, u32[]{:S(2)}, u32[]{:S(2)}) %collective-permute-start.5) | collective-permute-done | bytes 18464 | tf_op jit(solution)/shard_map/ppermute | solution.py:40
  54.9 10.6 %update.3 = (f32[48,108,512]{2,1,0:T(8,128)S(1)}, f32[48,1,128]{2,1,0:T(1,128)S(1)}) custom-call(f32[1,108,512]{2,1,0:T(8,128)S(1)} %collective-permute-done.above, f32[48,108,512]{2,1,0:T(8,128)S(1)} %bitcast.238, f32[48,108,512]{2,1,0:T(8,128)S(1)} %bitcast.239, f32[48,108,512]{2,1,0:T(8,128)S(1)} %bitcast.240, ...), custom_call_target="tpu_custom_call" | custom-call | tf_op jit(solution)/shard_map/update/pallas_call | solution.py:170
  65.5 4.2 %copy-done.4 = f32[48,108,512]{2,1,0:T(8,128)} copy-done((f32[48,108,512]{2,1,0:T(8,128)}, f32[48,108,512]{2,1,0:T(8,128)S(1)}, u32[]{:S(2)}) %copy-start.4) | copy-done | bytes 10616856
  71.3 2.0 collective-permute-done.6
  74.8 2.0 collective-permute-done.7
  78.0 2.5 collective-permute-start.9
  82.0 3.0 %collective-permute-start.10 = (f32[1,128]{1,0:T(1,128)S(1)}, f32[1,128]{1,0:T(1,128)S(1)}, u32[]{:S(2)}, u32[]{:S(2)}) collective-permute-start(f32[1,128]{1,0:T(1,128)S(1)} %add.569), channel_id=1, source_target_pairs={{0,4},{1,5},{2,6},{3,7},{4,0},{5,1},{6,2},{7,3},{8,12},{9,13},{10,... | collective-permute-start | bytes 1544 | tf_op jit(solution)/shard_map/ppermute | solution.py:130
  87.8 11.8 %multiply_add_fusion.1.prev.mid_ref.nxt = f32[48,108,512]{2,1,0:T(8,128)S(1)} fusion(f32[48,108,512]{2,1,0:T(8,128)} %copy-done.4, f32[]{:T(128)S(6)} %div.107, f32[108,48,512]{2,1,0:T(8,128)} %param.1), kind=kLoop, calls=%fused_computation.3 | loop fusion | flops 5308416 | bytes 31850500 | tf_op jit(solution)/shard_map/add | solution.py:172
  101.0 3.0 %collective-permute-start.11 = (f32[1,108,512]{2,1,0:T(8,128)S(1)}, f32[1,108,512]{2,1,0:T(8,128)S(1)}, u32[]{:S(2)}, u32[]{:S(2)}) collective-permute-start(f32[1,108,512]{2,1,0:T(8,128)S(1)} %get-tuple-element.22), channel_id=1, source_target_pairs={{0,1},{1,2},{2,3},{3,4},{4,5},{5,6},{6,7},{8,9},{9,10},{10,11},{11... | collective-permute-start | bytes 663560 | tf_op jit(solution)/shard_map/ppermute | solution.py:160
  105.2 10.5 %tensor.4 = f32[48,3,512]{2,1,0:T(4,128)S(1)} custom-call(f32[1,108,512]{2,1,0:T(8,128)S(1)} %collective-permute-done.11.above, f32[48,108,512]{2,1,0:T(8,128)S(1)} %multiply_add_fusion.1.prev.mid_ref.nxt, f32[48,108,512]{2,1,0:T(8,128)S(1)} %multiply_add_fusion.1.prev.mid_ref.nxt, f32[48,108,512]{2,1,0:T(8,128)S(1)} %multiply_add_fusion.1.prev.mid_ref.nxt, ...), custom_call_target="tpu_custom_call" | custom-call | tf_op jit(solution)/shard_map/tensor/pallas_call | solution.py:162
  115.7 1.6 collective-permute-start.13
  117.3 5.9 %collective-permute-done.13 = f32[3,48,512]{2,1,0:T(8,128)S(1)} collective-permute-done((f32[3,48,512]{2,1,0:T(8,128)S(1)}, f32[3,48,512]{2,1,0:T(8,128)S(1)}, u32[]{:S(2)}, u32[]{:S(2)}) %collective-permute-start.13) | collective-permute-done | bytes 294944 | tf_op jit(solution)/shard_map/ppermute | solution.py:130
  123.3 1.6 collective-permute-start.14
  124.9 7.0 %collective-permute-done.14 = f32[3,48,512]{2,1,0:T(8,128)S(1)} collective-permute-done((f32[3,48,512]{2,1,0:T(8,128)S(1)}, f32[3,48,512]{2,1,0:T(8,128)S(1)}, u32[]{:S(2)}, u32[]{:S(2)}) %collective-permute-start.14) | collective-permute-done | bytes 294944 | tf_op jit(solution)/shard_map/ppermute | solution.py:130
  132.0 3.1 %collective-permute-start.15 = (f32[3,3,512]{2,1,0:T(4,128)S(1)}, f32[3,3,512]{2,1,0:T(4,128)S(1)}, u32[]{:S(2)}, u32[]{:S(2)}) collective-permute-start(f32[3,3,512]{2,1,0:T(4,128)S(1)} %get-tuple-element.34), channel_id=1, source_target_pairs={{0,1},{1,2},{2,3},{3,4},{4,5},{5,6},{6,7},{8,9},{9,10},{10,11},{11... | collective-permute-start | bytes 55304 | tf_op jit(solution)/shard_map/ppermute | solution.py:38
  136.4 5.4 %collective-permute-done.16 = f32[3,3,512]{2,1,0:T(4,128)S(1)} collective-permute-done((f32[3,3,512]{2,1,0:T(4,128)S(1)}, f32[3,3,512]{2,1,0:T(4,128)S(1)}, u32[]{:S(2)}, u32[]{:S(2)}) %collective-permute-start.16) | collective-permute-done | bytes 18464 | tf_op jit(solution)/shard_map/ppermute | solution.py:40
  143.6 11.1 %update.4 = (f32[48,108,512]{2,1,0:T(8,128)S(1)}, f32[48,1,128]{2,1,0:T(1,128)S(1)}) custom-call(f32[1,108,512]{2,1,0:T(8,128)S(1)} %collective-permute-done.11.above, f32[48,108,512]{2,1,0:T(8,128)S(1)} %multiply_add_fusion.1.prev.mid_ref.nxt, f32[48,108,512]{2,1,0:T(8,128)S(1)} %multiply_add_fusion.1.prev.mid_ref.nxt, ...), custom_call_target="tpu_custom_call" | custom-call | tf_op jit(solution)/shard_map/update/pallas_call | solution.py:170
  154.8 4.0 %copy-done.5 = f32[48,108,512]{2,1,0:T(8,128)} copy-done((f32[48,108,512]{2,1,0:T(8,128)}, f32[48,108,512]{2,1,0:T(8,128)S(1)}, u32[]{:S(2)}) %copy-start.5) | copy-done | bytes 10616856
  160.4 2.0 collective-permute-done.17
  164.0 2.0 collective-permute-done.18
  167.1 2.5 collective-permute-start.20
  172.5 3.1 %collective-permute-done.21 = f32[1,128]{1,0:T(1,128)S(1)} collective-permute-done((f32[1,128]{1,0:T(1,128)S(1)}, f32[1,128]{1,0:T(1,128)S(1)}, u32[]{:S(2)}, u32[]{:S(2)}) %collective-permute-start.21) | collective-permute-done | bytes 544 | tf_op jit(solution)/shard_map/ppermute | solution.py:130
  176.9 8.5 %multiply_add_fusion.prev.mid_ref.nxt = f32[48,108,512]{2,1,0:T(8,128)S(1)} fusion(f32[48,108,512]{2,1,0:T(8,128)} %copy-done.2, f32[48,108,512]{2,1,0:T(8,128)} %copy-done.5, f32[]{:T(128)S(6)} %div.113), kind=kLoop, calls=%fused_computation.2 | loop fusion | flops 5308416 | bytes 31850500 | tf_op jit(solution)/shard_map/add | solution.py:172
  186.7 3.0 %collective-permute-start.22 = (f32[1,108,512]{2,1,0:T(8,128)S(1)}, f32[1,108,512]{2,1,0:T(8,128)S(1)}, u32[]{:S(2)}, u32[]{:S(2)}) collective-permute-start(f32[1,108,512]{2,1,0:T(8,128)S(1)} %get-tuple-element.20), channel_id=1, source_target_pairs={{0,1},{1,2},{2,3},{3,4},{4,5},{5,6},{6,7},{8,9},{9,10},{10,11},{11... | collective-permute-start | bytes 663560 | tf_op jit(solution)/shard_map/ppermute | solution.py:160
  190.8 10.2 %tensor.5 = f32[48,3,512]{2,1,0:T(4,128)S(1)} custom-call(f32[1,108,512]{2,1,0:T(8,128)S(1)} %collective-permute-done.22.above, f32[48,108,512]{2,1,0:T(8,128)S(1)} %multiply_add_fusion.prev.mid_ref.nxt, f32[48,108,512]{2,1,0:T(8,128)S(1)} %multiply_add_fusion.prev.mid_ref.nxt, f32[48,108,512]{2,1,0:T(8,128)S(1)} %multiply_add_fusion.prev.mid_ref.nxt, ...), custom_call_target="tpu_custom_call" | custom-call | tf_op jit(solution)/shard_map/tensor/pallas_call | solution.py:162
  202.7 5.8 %collective-permute-done.24 = f32[3,48,512]{2,1,0:T(8,128)S(1)} collective-permute-done((f32[3,48,512]{2,1,0:T(8,128)S(1)}, f32[3,48,512]{2,1,0:T(8,128)S(1)}, u32[]{:S(2)}, u32[]{:S(2)}) %collective-permute-start.24) | collective-permute-done | bytes 294944 | tf_op jit(solution)/shard_map/ppermute | solution.py:130
  208.7 1.6 collective-permute-start.25
  210.2 6.9 %collective-permute-done.25 = f32[3,48,512]{2,1,0:T(8,128)S(1)} collective-permute-done((f32[3,48,512]{2,1,0:T(8,128)S(1)}, f32[3,48,512]{2,1,0:T(8,128)S(1)}, u32[]{:S(2)}, u32[]{:S(2)}) %collective-permute-start.25) | collective-permute-done | bytes 294944 | tf_op jit(solution)/shard_map/ppermute | solution.py:130
  217.2 3.2 %collective-permute-start.26 = (f32[3,3,512]{2,1,0:T(4,128)S(1)}, f32[3,3,512]{2,1,0:T(4,128)S(1)}, u32[]{:S(2)}, u32[]{:S(2)}) collective-permute-start(f32[3,3,512]{2,1,0:T(4,128)S(1)} %get-tuple-element.30), channel_id=1, source_target_pairs={{0,1},{1,2},{2,3},{3,4},{4,5},{5,6},{6,7},{8,9},{9,10},{10,11},{11... | collective-permute-start | bytes 55304 | tf_op jit(solution)/shard_map/ppermute | solution.py:38
  221.9 3.7 %collective-permute-done.27 = f32[3,3,512]{2,1,0:T(4,128)S(1)} collective-permute-done((f32[3,3,512]{2,1,0:T(4,128)S(1)}, f32[3,3,512]{2,1,0:T(4,128)S(1)}, u32[]{:S(2)}, u32[]{:S(2)}) %collective-permute-start.27) | collective-permute-done | bytes 18464 | tf_op jit(solution)/shard_map/ppermute | solution.py:40
  228.8 4.1 %copy-done.1 = f32[48,108,512]{2,1,0:T(8,128)S(1)} copy-done((f32[48,108,512]{2,1,0:T(8,128)S(1)}, f32[48,108,512]{2,1,0:T(8,128)}, u32[]{:S(2)}) %copy-start.1) | copy-done | bytes 10616856
  233.0 10.2 %update.5 = (f32[48,108,512]{2,1,0:T(8,128)S(1)}, f32[48,1,128]{2,1,0:T(1,128)S(1)}) custom-call(f32[1,108,512]{2,1,0:T(8,128)S(1)} %collective-permute-done.22.above, f32[48,108,512]{2,1,0:T(8,128)S(1)} %copy-done.1, f32[48,108,512]{2,1,0:T(8,128)S(1)} %copy-done.1, f32[48,108,512]{2,1,0:T(8,128)S(1)} %copy-done.1, ...), custom_call_target="tpu_custom_call" | custom-call | tf_op jit(solution)/shard_map/update/pallas_call | solution.py:170
  243.2 4.0 %copy-done.3 = f32[48,108,512]{2,1,0:T(8,128)} copy-done((f32[48,108,512]{2,1,0:T(8,128)}, f32[48,108,512]{2,1,0:T(8,128)S(1)}, u32[]{:S(2)}) %copy-start.3) | copy-done | bytes 10616856
  248.8 2.0 collective-permute-done.28
  252.4 2.0 collective-permute-done.29
  255.5 2.5 collective-permute-start.31
  259.5 1.6 collective-permute-start.32
  261.1 2.8 collective-permute-done.32
  265.2 8.6 %add_bitcast_fusion = f32[108,48,512]{2,0,1:T(8,128)S(1)} fusion(f32[48,108,512]{2,1,0:T(8,128)} %copy-done, f32[48,108,512]{2,1,0:T(8,128)} %copy-done.3, f32[]{:T(128)S(6)} %div.119), kind=kLoop, calls=%fused_computation.1 | loop fusion | flops 5308416 | bytes 31850500 | tf_op jit(solution)/shard_map/transpose | solution.py:173
  273.8 10.3 %copy.43 = f32[108,48,512]{2,1,0:T(8,128)} copy(f32[108,48,512]{2,0,1:T(8,128)S(1)} %add_bitcast_fusion) | data formatting | bytes 21233664 | tf_op jit(solution)/shard_map/transpose | solution.py:173
  (115 shorter events, 42.5 us)
Async XLA Ops:
  10.2 4.4 %collective-permute-start.1 = (f32[1,108,512]{2,1,0:T(8,128)S(1)}, f32[1,108,512]{2,1,0:T(8,128)S(1)}, u32[]{:S(2)}, u32[]{:S(2)}) collective-permute-start(f32[1,108,512]{2,1,0:T(8,128)S(1)} %get-tuple-element.23), channel_id=1, source_target_pairs={{1,0},{2,1},{3,2},{4,3},{5,4},{6,5},{7,6},{9,8},{10,9},{11,10},{12... | collective-permute-start | bytes 663560 | tf_op jit(solution)/shard_map/ppermute | solution.py:161
  11.5 4.1 %collective-permute-start = (f32[1,108,512]{2,1,0:T(8,128)S(1)}, f32[1,108,512]{2,1,0:T(8,128)S(1)}, u32[]{:S(2)}, u32[]{:S(2)}) collective-permute-start(f32[1,108,512]{2,1,0:T(8,128)S(1)} %get-tuple-element.24), channel_id=1, source_target_pairs={{0,1},{1,2},{2,3},{3,4},{4,5},{5,6},{6,7},{8,9},{9,10},{10,11},{11... | collective-permute-start | bytes 663560 | tf_op jit(solution)/shard_map/ppermute | solution.py:160
  26.0 8.3 %collective-permute-start.2 = (f32[3,48,512]{2,1,0:T(8,128)S(1)}, f32[3,48,512]{2,1,0:T(8,128)S(1)}, u32[]{:S(2)}, u32[]{:S(2)}) collective-permute-start(f32[3,48,512]{2,1,0:T(8,128)S(1)} %bitcast.241), channel_id=1, source_target_pairs={{0,8},{8,0},{16,24},{24,16},{1,9},{9,1},{17,25},{25,17},{2,10},{10... | collective-permute-start | bytes 884744 | tf_op jit(solution)/shard_map/ppermute | solution.py:130
  34.3 9.1 %collective-permute-start.3 = (f32[3,48,512]{2,1,0:T(8,128)S(1)}, f32[3,48,512]{2,1,0:T(8,128)S(1)}, u32[]{:S(2)}, u32[]{:S(2)}) collective-permute-start(f32[3,48,512]{2,1,0:T(8,128)S(1)} %fusion.139), channel_id=1, source_target_pairs={{0,16},{8,24},{16,0},{24,8},{1,17},{9,25},{17,1},{25,9},{2,18},{10... | collective-permute-start | bytes 884744 | tf_op jit(solution)/shard_map/ppermute | solution.py:130
  43.5 4.5 %collective-permute-start.4 = (f32[3,3,512]{2,1,0:T(4,128)S(1)}, f32[3,3,512]{2,1,0:T(4,128)S(1)}, u32[]{:S(2)}, u32[]{:S(2)}) collective-permute-start(f32[3,3,512]{2,1,0:T(4,128)S(1)} %get-tuple-element.38), channel_id=1, source_target_pairs={{0,1},{1,2},{2,3},{3,4},{4,5},{5,6},{6,7},{8,9},{9,10},{10,11},{11... | collective-permute-start | bytes 55304 | tf_op jit(solution)/shard_map/ppermute | solution.py:38
  46.6 6.5 %collective-permute-start.5 = (f32[3,3,512]{2,1,0:T(4,128)S(1)}, f32[3,3,512]{2,1,0:T(4,128)S(1)}, u32[]{:S(2)}, u32[]{:S(2)}) collective-permute-start(f32[3,3,512]{2,1,0:T(4,128)S(1)} %get-tuple-element.39), channel_id=1, source_target_pairs={{1,0},{2,1},{3,2},{4,3},{5,4},{6,5},{7,6},{9,8},{10,9},{11,10},{12... | collective-permute-start | bytes 55304 | tf_op jit(solution)/shard_map/ppermute | solution.py:40
  65.5 4.2 %copy-start.4 = (f32[48,108,512]{2,1,0:T(8,128)}, f32[48,108,512]{2,1,0:T(8,128)S(1)}, u32[]{:S(2)}) copy-start(f32[48,108,512]{2,1,0:T(8,128)S(1)} %get-tuple-element.12) | copy-start | bytes 31850500
  69.7 3.6 %collective-permute-start.6 = (f32[1,128]{1,0:T(1,128)S(1)}, f32[1,128]{1,0:T(1,128)S(1)}, u32[]{:S(2)}, u32[]{:S(2)}) collective-permute-start(f32[1,128]{1,0:T(1,128)S(1)} %bitcast.245), channel_id=1, source_target_pairs={{0,8},{8,0},{16,24},{24,16},{1,9},{9,1},{17,25},{25,17},{2,10},{10... | collective-permute-start | bytes 1544 | tf_op jit(solution)/shard_map/ppermute | solution.py:130
  73.3 3.5 %collective-permute-start.7 = (f32[1,128]{1,0:T(1,128)S(1)}, f32[1,128]{1,0:T(1,128)S(1)}, u32[]{:S(2)}, u32[]{:S(2)}) collective-permute-start(f32[1,128]{1,0:T(1,128)S(1)} %bitcast_add_fusion.6), channel_id=1, source_target_pairs={{0,16},{8,24},{16,0},{24,8},{1,17},{9,25},{17,1},{25,9},{2,18},{10... | collective-permute-start | bytes 1544 | tf_op jit(solution)/shard_map/ppermute | solution.py:130
  76.9 1.1 collective-permute-start.8
  78.0 4.0 %collective-permute-start.9 = (f32[1,128]{1,0:T(1,128)S(1)}, f32[1,128]{1,0:T(1,128)S(1)}, u32[]{:S(2)}, u32[]{:S(2)}) collective-permute-start(f32[1,128]{1,0:T(1,128)S(1)} %add.568), channel_id=1, source_target_pairs={{0,2},{1,3},{2,0},{3,1},{4,6},{5,7},{6,4},{7,5},{8,10},{9,11},{10,... | collective-permute-start | bytes 1544 | tf_op jit(solution)/shard_map/ppermute | solution.py:130
  82.0 4.6 %collective-permute-start.10 = (f32[1,128]{1,0:T(1,128)S(1)}, f32[1,128]{1,0:T(1,128)S(1)}, u32[]{:S(2)}, u32[]{:S(2)}) collective-permute-start(f32[1,128]{1,0:T(1,128)S(1)} %add.569), channel_id=1, source_target_pairs={{0,4},{1,5},{2,6},{3,7},{4,0},{5,1},{6,2},{7,3},{8,12},{9,13},{10,... | collective-permute-start | bytes 1544 | tf_op jit(solution)/shard_map/ppermute | solution.py:130
  99.7 43.9 %copy-start.2 = (f32[48,108,512]{2,1,0:T(8,128)}, f32[48,108,512]{2,1,0:T(8,128)S(1)}, u32[]{:S(2)}) copy-start(f32[48,108,512]{2,1,0:T(8,128)S(1)} %multiply_add_fusion.1.prev.mid_ref.nxt) | copy-start | bytes 31850500
  99.7 4.4 %collective-permute-start.12 = (f32[1,108,512]{2,1,0:T(8,128)S(1)}, f32[1,108,512]{2,1,0:T(8,128)S(1)}, u32[]{:S(2)}, u32[]{:S(2)}) collective-permute-start(f32[1,108,512]{2,1,0:T(8,128)S(1)} %get-tuple-element.21), channel_id=1, source_target_pairs={{1,0},{2,1},{3,2},{4,3},{5,4},{6,5},{7,6},{9,8},{10,9},{11,10},{12... | collective-permute-start | bytes 663560 | tf_op jit(solution)/shard_map/ppermute | solution.py:161
  101.0 4.1 %collective-permute-start.11 = (f32[1,108,512]{2,1,0:T(8,128)S(1)}, f32[1,108,512]{2,1,0:T(8,128)S(1)}, u32[]{:S(2)}, u32[]{:S(2)}) collective-permute-start(f32[1,108,512]{2,1,0:T(8,128)S(1)} %get-tuple-element.22), channel_id=1, source_target_pairs={{0,1},{1,2},{2,3},{3,4},{4,5},{5,6},{6,7},{8,9},{9,10},{10,11},{11... | collective-permute-start | bytes 663560 | tf_op jit(solution)/shard_map/ppermute | solution.py:160
  115.7 7.5 %collective-permute-start.13 = (f32[3,48,512]{2,1,0:T(8,128)S(1)}, f32[3,48,512]{2,1,0:T(8,128)S(1)}, u32[]{:S(2)}, u32[]{:S(2)}) collective-permute-start(f32[3,48,512]{2,1,0:T(8,128)S(1)} %bitcast.242), channel_id=1, source_target_pairs={{0,8},{8,0},{16,24},{24,16},{1,9},{9,1},{17,25},{25,17},{2,10},{10... | collective-permute-start | bytes 884744 | tf_op jit(solution)/shard_map/ppermute | solution.py:130
  123.3 8.6 %collective-permute-start.14 = (f32[3,48,512]{2,1,0:T(8,128)S(1)}, f32[3,48,512]{2,1,0:T(8,128)S(1)}, u32[]{:S(2)}, u32[]{:S(2)}) collective-permute-start(f32[3,48,512]{2,1,0:T(8,128)S(1)} %fusion.138), channel_id=1, source_target_pairs={{0,16},{8,24},{16,0},{24,8},{1,17},{9,25},{17,1},{25,9},{2,18},{10... | collective-permute-start | bytes 884744 | tf_op jit(solution)/shard_map/ppermute | solution.py:130
  132.0 4.4 %collective-permute-start.15 = (f32[3,3,512]{2,1,0:T(4,128)S(1)}, f32[3,3,512]{2,1,0:T(4,128)S(1)}, u32[]{:S(2)}, u32[]{:S(2)}) collective-permute-start(f32[3,3,512]{2,1,0:T(4,128)S(1)} %get-tuple-element.34), channel_id=1, source_target_pairs={{0,1},{1,2},{2,3},{3,4},{4,5},{5,6},{6,7},{8,9},{9,10},{10,11},{11... | collective-permute-start | bytes 55304 | tf_op jit(solution)/shard_map/ppermute | solution.py:38
  135.1 6.7 %collective-permute-start.16 = (f32[3,3,512]{2,1,0:T(4,128)S(1)}, f32[3,3,512]{2,1,0:T(4,128)S(1)}, u32[]{:S(2)}, u32[]{:S(2)}) collective-permute-start(f32[3,3,512]{2,1,0:T(4,128)S(1)} %get-tuple-element.35), channel_id=1, source_target_pairs={{1,0},{2,1},{3,2},{4,3},{5,4},{6,5},{7,6},{9,8},{10,9},{11,10},{12... | collective-permute-start | bytes 55304 | tf_op jit(solution)/shard_map/ppermute | solution.py:40
  154.8 4.0 %copy-start.5 = (f32[48,108,512]{2,1,0:T(8,128)}, f32[48,108,512]{2,1,0:T(8,128)S(1)}, u32[]{:S(2)}) copy-start(f32[48,108,512]{2,1,0:T(8,128)S(1)} %get-tuple-element.14) | copy-start | bytes 31850500
  158.9 3.6 %collective-permute-start.17 = (f32[1,128]{1,0:T(1,128)S(1)}, f32[1,128]{1,0:T(1,128)S(1)}, u32[]{:S(2)}, u32[]{:S(2)}) collective-permute-start(f32[1,128]{1,0:T(1,128)S(1)} %bitcast.246), channel_id=1, source_target_pairs={{0,8},{8,0},{16,24},{24,16},{1,9},{9,1},{17,25},{25,17},{2,10},{10... | collective-permute-start | bytes 1544 | tf_op jit(solution)/shard_map/ppermute | solution.py:130
  162.5 3.5 %collective-permute-start.18 = (f32[1,128]{1,0:T(1,128)S(1)}, f32[1,128]{1,0:T(1,128)S(1)}, u32[]{:S(2)}, u32[]{:S(2)}) collective-permute-start(f32[1,128]{1,0:T(1,128)S(1)} %bitcast_add_fusion.5), channel_id=1, source_target_pairs={{0,16},{8,24},{16,0},{24,8},{1,17},{9,25},{17,1},{25,9},{2,18},{10... | collective-permute-start | bytes 1544 | tf_op jit(solution)/shard_map/ppermute | solution.py:130
  166.0 1.1 collective-permute-start.19
  167.1 4.0 %collective-permute-start.20 = (f32[1,128]{1,0:T(1,128)S(1)}, f32[1,128]{1,0:T(1,128)S(1)}, u32[]{:S(2)}, u32[]{:S(2)}) collective-permute-start(f32[1,128]{1,0:T(1,128)S(1)} %add.601), channel_id=1, source_target_pairs={{0,2},{1,3},{2,0},{3,1},{4,6},{5,7},{6,4},{7,5},{8,10},{9,11},{10,... | collective-permute-start | bytes 1544 | tf_op jit(solution)/shard_map/ppermute | solution.py:130
  171.1 4.4 %collective-permute-start.21 = (f32[1,128]{1,0:T(1,128)S(1)}, f32[1,128]{1,0:T(1,128)S(1)}, u32[]{:S(2)}, u32[]{:S(2)}) collective-permute-start(f32[1,128]{1,0:T(1,128)S(1)} %add.602), channel_id=1, source_target_pairs={{0,4},{1,5},{2,6},{3,7},{4,0},{5,1},{6,2},{7,3},{8,12},{9,13},{10,... | collective-permute-start | bytes 1544 | tf_op jit(solution)/shard_map/ppermute | solution.py:130
  185.3 15.7 %copy-start = (f32[48,108,512]{2,1,0:T(8,128)}, f32[48,108,512]{2,1,0:T(8,128)S(1)}, u32[]{:S(2)}) copy-start(f32[48,108,512]{2,1,0:T(8,128)S(1)} %multiply_add_fusion.prev.mid_ref.nxt) | copy-start | bytes 31850500
  185.4 4.4 %collective-permute-start.23 = (f32[1,108,512]{2,1,0:T(8,128)S(1)}, f32[1,108,512]{2,1,0:T(8,128)S(1)}, u32[]{:S(2)}, u32[]{:S(2)}) collective-permute-start(f32[1,108,512]{2,1,0:T(8,128)S(1)} %get-tuple-element.19), channel_id=1, source_target_pairs={{1,0},{2,1},{3,2},{4,3},{5,4},{6,5},{7,6},{9,8},{10,9},{11,10},{12... | collective-permute-start | bytes 663560 | tf_op jit(solution)/shard_map/ppermute | solution.py:161
  186.7 4.1 %collective-permute-start.22 = (f32[1,108,512]{2,1,0:T(8,128)S(1)}, f32[1,108,512]{2,1,0:T(8,128)S(1)}, u32[]{:S(2)}, u32[]{:S(2)}) collective-permute-start(f32[1,108,512]{2,1,0:T(8,128)S(1)} %get-tuple-element.20), channel_id=1, source_target_pairs={{0,1},{1,2},{2,3},{3,4},{4,5},{5,6},{6,7},{8,9},{9,10},{10,11},{11... | collective-permute-start | bytes 663560 | tf_op jit(solution)/shard_map/ppermute | solution.py:160
  201.2 7.4 %collective-permute-start.24 = (f32[3,48,512]{2,1,0:T(8,128)S(1)}, f32[3,48,512]{2,1,0:T(8,128)S(1)}, u32[]{:S(2)}, u32[]{:S(2)}) collective-permute-start(f32[3,48,512]{2,1,0:T(8,128)S(1)} %bitcast.243), channel_id=1, source_target_pairs={{0,8},{8,0},{16,24},{24,16},{1,9},{9,1},{17,25},{25,17},{2,10},{10... | collective-permute-start | bytes 884744 | tf_op jit(solution)/shard_map/ppermute | solution.py:130
  208.7 8.4 %collective-permute-start.25 = (f32[3,48,512]{2,1,0:T(8,128)S(1)}, f32[3,48,512]{2,1,0:T(8,128)S(1)}, u32[]{:S(2)}, u32[]{:S(2)}) collective-permute-start(f32[3,48,512]{2,1,0:T(8,128)S(1)} %fusion.137), channel_id=1, source_target_pairs={{0,16},{8,24},{16,0},{24,8},{1,17},{9,25},{17,1},{25,9},{2,18},{10... | collective-permute-start | bytes 884744 | tf_op jit(solution)/shard_map/ppermute | solution.py:130
  217.2 4.8 %collective-permute-start.26 = (f32[3,3,512]{2,1,0:T(4,128)S(1)}, f32[3,3,512]{2,1,0:T(4,128)S(1)}, u32[]{:S(2)}, u32[]{:S(2)}) collective-permute-start(f32[3,3,512]{2,1,0:T(4,128)S(1)} %get-tuple-element.30), channel_id=1, source_target_pairs={{0,1},{1,2},{2,3},{3,4},{4,5},{5,6},{6,7},{8,9},{9,10},{10,11},{11... | collective-permute-start | bytes 55304 | tf_op jit(solution)/shard_map/ppermute | solution.py:38
  220.4 5.2 %collective-permute-start.27 = (f32[3,3,512]{2,1,0:T(4,128)S(1)}, f32[3,3,512]{2,1,0:T(4,128)S(1)}, u32[]{:S(2)}, u32[]{:S(2)}) collective-permute-start(f32[3,3,512]{2,1,0:T(4,128)S(1)} %get-tuple-element.31), channel_id=1, source_target_pairs={{1,0},{2,1},{3,2},{4,3},{5,4},{6,5},{7,6},{9,8},{10,9},{11,10},{12... | collective-permute-start | bytes 55304 | tf_op jit(solution)/shard_map/ppermute | solution.py:40
  228.8 4.1 %copy-start.1 = (f32[48,108,512]{2,1,0:T(8,128)S(1)}, f32[48,108,512]{2,1,0:T(8,128)}, u32[]{:S(2)}) copy-start(f32[48,108,512]{2,1,0:T(8,128)} %copy-done) | copy-start | bytes 31850500
  243.2 4.0 %copy-start.3 = (f32[48,108,512]{2,1,0:T(8,128)}, f32[48,108,512]{2,1,0:T(8,128)S(1)}, u32[]{:S(2)}) copy-start(f32[48,108,512]{2,1,0:T(8,128)S(1)} %get-tuple-element.16) | copy-start | bytes 31850500
  247.3 3.6 %collective-permute-start.28 = (f32[1,128]{1,0:T(1,128)S(1)}, f32[1,128]{1,0:T(1,128)S(1)}, u32[]{:S(2)}, u32[]{:S(2)}) collective-permute-start(f32[1,128]{1,0:T(1,128)S(1)} %bitcast.244), channel_id=1, source_target_pairs={{0,8},{8,0},{16,24},{24,16},{1,9},{9,1},{17,25},{25,17},{2,10},{10... | collective-permute-start | bytes 1544 | tf_op jit(solution)/shard_map/ppermute | solution.py:130
  250.9 3.5 %collective-permute-start.29 = (f32[1,128]{1,0:T(1,128)S(1)}, f32[1,128]{1,0:T(1,128)S(1)}, u32[]{:S(2)}, u32[]{:S(2)}) collective-permute-start(f32[1,128]{1,0:T(1,128)S(1)} %bitcast_add_fusion.4), channel_id=1, source_target_pairs={{0,16},{8,24},{16,0},{24,8},{1,17},{9,25},{17,1},{25,9},{2,18},{10... | collective-permute-start | bytes 1544 | tf_op jit(solution)/shard_map/ppermute | solution.py:130
  254.4 1.1 collective-permute-start.30
  255.5 4.0 %collective-permute-start.31 = (f32[1,128]{1,0:T(1,128)S(1)}, f32[1,128]{1,0:T(1,128)S(1)}, u32[]{:S(2)}, u32[]{:S(2)}) collective-permute-start(f32[1,128]{1,0:T(1,128)S(1)} %add.634), channel_id=1, source_target_pairs={{0,2},{1,3},{2,0},{3,1},{4,6},{5,7},{6,4},{7,5},{8,10},{9,11},{10,... | collective-permute-start | bytes 1544 | tf_op jit(solution)/shard_map/ppermute | solution.py:130
  259.5 4.4 %collective-permute-start.32 = (f32[1,128]{1,0:T(1,128)S(1)}, f32[1,128]{1,0:T(1,128)S(1)}, u32[]{:S(2)}, u32[]{:S(2)}) collective-permute-start(f32[1,128]{1,0:T(1,128)S(1)} %add.635), channel_id=1, source_target_pairs={{0,4},{1,5},{2,6},{3,7},{4,0},{5,1},{6,2},{7,3},{8,12},{9,13},{10,... | collective-permute-start | bytes 1544 | tf_op jit(solution)/shard_map/ppermute | solution.py:130
